TPU v7x, 768 devices: a whole 4x8x12 slice. The times are simulated.
768 devices in a mesh: row: 96 (over x, z, core), col: 8 (over y).
Axes of the slice: x: 4, y: 8, z: 12, core: 2. Of those that a mesh axis runs over, the one named last changes fastest.
Arguments:
- values: float32 [12288, 1024], P('row', 'col'), may hold values from -0.66 to 0.66
- column_ids: int32 [192, 16], P('row', 'col'), may hold values from 0 to 23, as said below
- counts: int32 [192, 8], P('row', 'col'), may hold values from 1 to 2
- keep_pattern: int32 [192, 192], P('row', 'col'), may hold values 0 or 1
Outputs:
- square: float32 [12288, 12288], P('row', 'col')
- purified: float32 [12288, 12288], P('row', 'col')
Inputs may be any that keep to these rules, and one draw needn't show every extreme that they name: `column_ids`: within one block row and panel the live slots name distinct block columns.
All inputs are finite; a program needn't handle non-finite values. No bound on the sum of `keep_pattern` on one device may be relied on, other than what follows from the above.
Results may differ from a plain program's by a relative error of at most 0.00008.
Values sent between devices are 32-bit elements; how exact they have to be, the bound alone decides.
A program may use at most 64 MiB of HBM per device.

v0:
```python
import jax
import jax.numpy as jnp
from jax import lax
from jax.sharding import PartitionSpec as P


def make_folder(left, slots, width, panel_cols, carry, piece):
    tiles, ids, live_counts = piece
    piece_rows = tiles.shape[0]
    group_rows = max((d for d in range(1, min(piece_rows, 32) + 1) if piece_rows % d == 0))
    turn_count = piece_rows // group_rows

    def add_group(turn_index, total):
        offset = turn_index * group_rows
        group_tiles = lax.dynamic_slice_in_dim(tiles, offset, group_rows, 0)
        group_ids = lax.dynamic_slice_in_dim(ids, offset, group_rows, 0)
        group_live = lax.dynamic_slice_in_dim(live_counts, offset, group_rows, 0)
        left_part = lax.dynamic_slice_in_dim(left, offset, group_rows, 1)
        blocks = group_tiles.reshape(group_rows, width, slots, width)
        product = jnp.einsum(
            "akb,kbsc->ksac",
            left_part,
            blocks,
            precision=lax.Precision.HIGHEST,
            preferred_element_type=jnp.float32,
        )
        placing = group_ids[:, :, None] == jnp.arange(panel_cols, dtype=jnp.int32)[None, None, :]
        placing = placing & (
            jnp.arange(slots, dtype=jnp.int32)[None, :, None] < group_live[:, None, None]
        )
        placed = jnp.einsum(
            "ksj,ksac->ajc",
            placing.astype(jnp.float32),
            product,
            precision=lax.Precision.HIGHEST,
            preferred_element_type=jnp.float32,
        )
        return total + placed

    return lax.fori_loop(0, turn_count, add_group, carry)


def local(values, column_ids, counts, keep_pattern):
    rows_here = column_ids.shape[0]
    slots = column_ids.shape[1]
    panel_cols = keep_pattern.shape[1]
    width = values.shape[1] // slots
    ncol = lax.axis_size("col")
    nblocks = rows_here * lax.axis_size("row")
    height = rows_here * width
    tiles = values.reshape(rows_here, width, slots * width)
    live_counts = counts.reshape(rows_here)
    row_tiles, row_ids, row_counts = (
        lax.all_gather(tiles[None], "col", axis=0, tiled=True),
        lax.all_gather(column_ids[None], "col", axis=0, tiled=True),
        lax.all_gather(live_counts[None], "col", axis=0, tiled=True),
    )
    global_ids = row_ids + (jnp.arange(ncol, dtype=jnp.int32) * panel_cols)[:, None, None]
    alive = jnp.arange(slots, dtype=jnp.int32)[None, None, :] < row_counts[:, :, None]
    onehot = (
        (global_ids[..., None] == jnp.arange(nblocks, dtype=jnp.int32)) & alive[..., None]
    ).astype(jnp.float32)
    row_blocks = row_tiles.reshape(ncol, rows_here, width, slots, width)
    left_first = jnp.einsum(
        "pisk,piasb->iakb",
        onehot,
        row_blocks,
        precision=lax.Precision.HIGHEST,
        preferred_element_type=jnp.float32,
    )
    left_first = left_first.reshape(height, nblocks, width)
    keep = jnp.repeat(keep_pattern.astype(jnp.float32), width, axis=0)[:, :, None]
    zeros_init = jnp.zeros((height, panel_cols, width), jnp.float32)
    first = make_folder(
        left_first,
        slots,
        width,
        panel_cols,
        zeros_init,
        (
            lax.all_gather(tiles, "row", axis=0, tiled=True),
            lax.all_gather(column_ids, "row", axis=0, tiled=True),
            lax.all_gather(live_counts, "row", axis=0, tiled=True),
        ),
    )
    square = (first * keep).reshape(height, panel_cols * width)
    square_row = lax.all_gather(square, "col", axis=1, tiled=True)
    left_second = square_row.reshape(height, nblocks, width)
    second = make_folder(
        left_second,
        slots,
        width,
        panel_cols,
        zeros_init,
        (
            lax.all_gather(tiles, "row", axis=0, tiled=True),
            lax.all_gather(column_ids, "row", axis=0, tiled=True),
            lax.all_gather(live_counts, "row", axis=0, tiled=True),
        ),
    )
    cube = (second * keep).reshape(height, panel_cols * width)
    return (square, 3.0 * square - 2.0 * cube)


def solution(mesh):
    return jax.shard_map(
        local,
        mesh=mesh,
        in_specs=(P("row", "col"), P("row", "col"), P("row", "col"), P("row", "col")),
        out_specs=(P("row", "col"), P("row", "col")),
        check_vma=False,
    )
```

profile of v0, /device:TPU:1, one launch (start us, length us, event | category | flops | bytes accessed | tf_op | source)
XLA Modules:
  0.0 521.1 jit_solution(7861681791288397355)
XLA Ops:
  12.7 12.0 %all-reduce = s32[16]{0:T(128)S(1)} all-reduce(s32[16]{0:T(128)S(1)} %get-tuple-element.343), channel_id=3, replica_groups=mesh['row'=96,'col'=8] {'col'}, use_global_device_ids=true, to_apply=%add | all-reduce | flops 16 | bytes 128
  24.9 11.0 %all-gather.3 = s32[8,2,2]{2,1,0:T(2,128)S(1)} all-gather(s32[1,2,2]{2,1,0:T(2,128)} %bitcast.101), channel_id=2, replica_groups=mesh['row'=96,'col'=8] {'col'}, dimensions={0}, use_global_device_ids=true | all-gather | bytes 144 | tf_op jit(solution)/shard_map/all_gather | solution.py:55
  36.0 20.7 %all_gather.27 = f32[8,2,64,128]{3,2,1,0:T(8,128)S(1)} all-gather(f32[1,2,64,128]{3,2,1,0:T(8,128)} %bitcast.100), channel_id=1, replica_groups=mesh['row'=96,'col'=8] {'col'}, dimensions={0}, use_global_device_ids=true | all-gather | bytes 589824 | tf_op jit(solution)/shard_map/all_gather | solution.py:54
  57.3 5.8 %fusion.32 = f32[2,192,64,64,1]{1,3,4,2,0:T(8,128)} fusion(f32[8,2,64,2,64]{4,3,2,1,0:T(2,128)S(1)} %reshape.102, s32[8,2,2]{0,2,1:T(2,128)S(1)} %broadcast_add_fusion, pred[8,2,2]{0,2,1:T(4,128)(4,1)S(1)} %iota_compare_fusion.5), kind=kOutput, calls=%fused_computation.32 | convolution fusion | flops 302002176 | bytes 6815904 | tf_op jit(solution)/shard_map/pisk,piasb->iakb/dot_general | solution.py:64
  63.1 8.4 %copy.47 = f32[128,192,64]{0,2,1:T(8,128)} copy(f32[128,192,64]{1,2,0:T(8,128)} %bitcast.94) | data formatting | bytes 12582912
  71.5 84.3 %all-gather.4 = s32[96,2,2]{2,1,0:T(2,128)S(1)} all-gather(s32[1,2,2]{2,1,0:T(2,128)S(1)} %bitcast.102), channel_id=1, replica_groups=mesh['row'=96,'col'=8] {'row'}, dimensions={0}, use_global_device_ids=true | all-gather | bytes 1552 | tf_op jit(solution)/shard_map/all_gather | solution.py:82
  156.2 185.1 %all-reduce.1 = s32[192]{0:T(256)S(1)} all-reduce(s32[192]{0:T(256)S(1)} %get-tuple-element.342), channel_id=4, replica_groups=mesh['row'=96,'col'=8] {'row'}, use_global_device_ids=true, to_apply=%add.1 | all-reduce | flops 192 | bytes 1536 | tf_op jit(solution)/shard_map/all_gather | solution.py:83
  341.4 9.6 %copy.46 = f32[192,64,128]{1,2,0:T(8,128)} copy(f32[192,64,128]{2,1,0:T(8,128)} %all-gather.8.cloned.1.call-done) | data formatting | bytes 12582912
  350.9 44.2 %while.28 = (s32[]{:T(128)}, f32[128,24,64]{0,1,2:T(8,128)S(1)}, f32[192,64,128]{1,2,0:T(8,128)}, f32[128,192,64]{0,2,1:T(8,128)}, s32[192,2]{0,1:T(2,128)S(1)},...) while((s32[]{:T(128)}, f32[128,24,64]{0,1,2:T(8,128)S(1)}, ...), condition=%wide.region_1.0_spmd.clone, body=%wide.region_0.0_spmd.clone.sunk | while | flops 554044480 | bytes 9962925 | solution.py:40
  350.9 1.7 constant_dynamic-slice_fusion.8
  352.7 3.2 convolution_bitcast_fusion.4
  356.1 2.2 fusion.56
  358.3 1.7 constant_dynamic-slice_fusion.8
  360.0 3.2 convolution_bitcast_fusion.4
  363.4 2.2 fusion.56
  365.7 1.7 constant_dynamic-slice_fusion.8
  367.4 3.2 convolution_bitcast_fusion.4
  370.8 2.2 fusion.56
  373.0 1.7 constant_dynamic-slice_fusion.8
  374.8 3.2 convolution_bitcast_fusion.4
  378.2 2.2 fusion.56
  380.4 1.7 constant_dynamic-slice_fusion.8
  382.1 3.2 convolution_bitcast_fusion.4
  385.5 2.2 fusion.56
  387.8 1.7 constant_dynamic-slice_fusion.8
  389.5 3.2 convolution_bitcast_fusion.4
  392.9 2.2 fusion.56
  396.2 2.3 copy.54
  398.5 69.2 %all-gather.10.cloned.1.call-done = f32[128,12288]{0,1:T(8,128)} async-done(((f32[128,1536]{0,1:T(8,128)}), f32[128,12288]{0,1:T(8,128)}) %all-gather.10.cloned.1.call-update) | async-done | bytes 6291472 | tf_op jit(solution)/shard_map/all_gather | solution.py:87
  467.7 44.2 %while.29 = (s32[]{:T(128)}, f32[128,24,64]{0,1,2:T(8,128)S(1)}, f32[192,64,128]{1,2,0:T(8,128)}, f32[128,192,64]{0,2,1:T(8,128)}, s32[192,2]{0,1:T(2,128)S(1)},...) while((s32[]{:T(128)}, f32[128,24,64]{0,1,2:T(8,128)S(1)}, ...), condition=%wide.region_3.0_spmd.clone, body=%wide.region_2.0_spmd.clone.sunk | while | flops 554044480 | bytes 9962925 | solution.py:40
  467.7 1.7 constant_dynamic-slice_fusion.10
  469.4 3.2 convolution_bitcast_fusion.5
  472.8 2.2 fusion.61
  475.0 1.7 constant_dynamic-slice_fusion.10
  476.8 3.2 convolution_bitcast_fusion.5
  480.2 2.2 fusion.61
  482.4 1.7 constant_dynamic-slice_fusion.10
  484.2 3.2 convolution_bitcast_fusion.5
  487.5 2.2 fusion.61
  489.8 1.7 constant_dynamic-slice_fusion.10
  491.5 3.2 convolution_bitcast_fusion.5
  494.9 2.2 fusion.61
  497.2 1.7 constant_dynamic-slice_fusion.10
  498.9 3.2 convolution_bitcast_fusion.5
  502.3 2.2 fusion.61
  504.5 1.7 constant_dynamic-slice_fusion.10
  506.3 3.2 convolution_bitcast_fusion.5
  509.6 2.2 fusion.61
  (70 shorter events, 10.7 us)
Async XLA Ops:
  7.2 334.2 %all-gather.8.cloned.1.call-start = ((), (), s32[]{:S(2)}) async-start(), calls=%async_computation | async-start | bytes 6356992 | tf_op jit(solution)/shard_map/all_gather | solution.py:81
  7.9 459.8 %all-gather.10.cloned.1.call-start = ((), (), s32[]{:S(2)}) async-start(), calls=%async_computation.1 | async-start | bytes 7077888 | tf_op jit(solution)/shard_map/all_gather | solution.py:87
  63.1 8.4 %copy-start.1 = (s32[2,2]{1,0:T(2,128)S(1)}, s32[2,2]{1,0:T(2,128)}, u32[]{:S(2)}) copy-start(s32[2,2]{1,0:T(2,128)} %param.9) | copy-start | bytes 52
  63.1 92.8 %copy-start.2 = (s32[2,24]{1,0:T(2,128)S(1)}, s32[2,24]{1,0:T(2,128)}, u32[]{:S(2)}) copy-start(s32[2,24]{1,0:T(2,128)} %param.11) | copy-start | bytes 580
  511.9 1.1 copy-start
Sparse Core Ops, SparseCore 0:
  11.7 127.9 all-gather.7
  396.3 71.3 all-gather.9
where the time goes:
time: 523 us; the launch traced here: 521 us
  blocking collectives  313 us (60%)
  matrix products  70.9 us (14%)
  waiting for transfers between devices  69.9 us (13%)
  local copies, waits for them, and re-layouts  49.6 us (9%)
  between operations  15.5 us (3%)
    all_gather x1, blocking collectives, local(): lax.all_gather(live_counts, 'row', axis=0, tiled=True)  185 us
    all_gather x1, blocking collectives, local(): lax.all_gather(column_ids, 'row', axis=0, tiled=True)  84.3 us
    all_gather x1, waiting for transfers between devices, local(): square_row = lax.all_gather(square, 'col', axis=1, tiled=True)  69.2 us
    dot_general x12, matrix products, add_group(): jnp.einsum('akb,kbsc->ksac', left_part, blocks, precision=lax.Precision.H...  38.5 us
    dot_general x12, matrix products, add_group(): jnp.einsum('ksj,ksac->ajc', placing.astype(jnp.float32), product, precisi...  26.7 us
    unnamed x16, local copies, waits for them, and re-layouts  25.8 us
    dynamic_slice x12, local copies, waits for them, and re-layouts, add_group(): group_tiles = lax.dynamic_slice_in_dim(tiles, offset, group_rows, 0)  20.8 us
    all_gather x1, blocking collectives, local(): lax.all_gather(tiles[None], 'col', axis=0, tiled=True)  20.7 us
  transfers between devices with their start and end apart: 2, of which 1 were waited for; matrix products, arithmetic and copies ran while one was open for 4% of the time, Pallas kernels for 0%

commit v1 on v0

v1 whole, which is shorter than its diff:
```python
import functools

import jax
import jax.numpy as jnp
from jax import lax
from jax.experimental import pallas as pl
from jax.experimental.pallas import tpu as pltpu
from jax.sharding import PartitionSpec as P

MESH = pl.DeviceIdType.MESH
NX, NZ, NY = 4, 12, 8
BLK = 64
TWO = 2 * BLK
NP = 4
CP = BLK // NP
EXTRA = 8
F32, BF16, I32 = jnp.float32, jnp.bfloat16, jnp.int32


def place():
    row, col = lax.axis_index("row"), lax.axis_index("col")
    return row // (2 * NZ), (row // 2) % NZ, row % 2, col


def to(x, z, core, y):
    return ((x * NZ + z) * 2 + core, y)


def greet(partners):
    barrier = pltpu.get_barrier_semaphore()
    for partner in partners:
        pl.semaphore_signal(barrier, inc=1, device_id=partner, device_id_type=MESH)
    pl.semaphore_wait(barrier, len(partners))


def copy(ref, send, recv, target):
    return pltpu.make_async_remote_copy(
        src_ref=ref, dst_ref=ref, send_sem=send, recv_sem=recv, device_id=target, device_id_type=MESH
    )


def split(a):
    high = a.astype(BF16)
    return high, (a - high.astype(F32)).astype(BF16)


def dot(a, b):
    return jnp.dot(a, b, preferred_element_type=F32)


def gather_panel(
    ids, counts, tile, panel, row, xs, xr, zs, zr, ss, sr, ys, yr
):
    x, z, core, y = place()
    west, east = (z + NZ - 1) % NZ, (z + 1) % NZ
    south, north = (y + NY - 1) % NY, (y + 1) % NY
    greet(
        [to((x + d) % NX, z, core, y) for d in range(1, NX)]
        + [to(x, west, core, y), to(x, east, core, y), to(x, z, 1 - core, y)]
        + [to(x, z, core, south), to(x, z, core, north)]
    )
    at_row = lax.broadcasted_iota(I32, (TWO, TWO), 0)
    at_lane = lax.broadcasted_iota(I32, (TWO, TWO), 1)
    live = jnp.where(at_row < BLK, counts[0, 0], counts[1, 0])
    held = jnp.where(at_lane // BLK < live, tile[...], 0.0).T
    lane = lax.broadcasted_iota(I32, (EXTRA, TWO), 1)
    tags = jnp.where(
        lane == 0, ids[0, 0], jnp.where(lane == 1, ids[0, 1], jnp.where(lane == 2, ids[1, 0], ids[1, 1]))
    ).astype(F32)
    row[y, :TWO] = held
    row[y, TWO:] = tags
    for h in range(NP):
        for s in range(2):
            at = (h * 2 + s) * CP
            panel[z, core, x, at : at + CP] = held[s * BLK + h * CP : s * BLK + (h + 1) * CP]
    panel[z, core, x, TWO:] = tags

    started = []

    def start(c):
        c.start()
        started.append(c)

    def y_copy(way, hop):
        slot = (y - hop) % NY if way == 0 else (y + hop) % NY
        return copy(row.at[slot], ys.at[way, hop], yr.at[way, hop], to(x, z, core, north if way == 0 else south))

    def z_copy(way, hop):
        slot = (z + NZ - hop) % NZ if way == 0 else (z + hop) % NZ
        return copy(panel.at[slot, core], zs.at[way, hop], zr.at[way, hop], to(x, east if way == 0 else west, core, y))

    def sibling(slot, n):
        return copy(panel.at[slot, core], ss.at[n], sr.at[n], to(x, z, 1 - core, y))

    y_hops, z_hops = (NY // 2, NY - 1 - NY // 2), (NZ // 2, NZ - 1 - NZ // 2)
    xc = []
    for d in range(1, NX):
        xc.append(copy(panel.at[z, core, x], xs.at[d - 1], xr.at[d - 1], to((x + d) % NX, z, core, y)))
        start(xc[-1])
    for way in range(2):
        if y_hops[way]:
            start(y_copy(way, 0))
    for c in xc:
        c.wait_recv()
    for way in range(2):
        if z_hops[way]:
            start(z_copy(way, 0))
    start(sibling(z, 0))
    for hop in range(1, max(NZ, NY) // 2 + 1):
        for way in range(2):
            if hop <= z_hops[way]:
                z_copy(way, hop - 1).wait_recv()
                if hop < z_hops[way]:
                    start(z_copy(way, hop))
                slot = (z + NZ - hop) % NZ if way == 0 else (z + hop) % NZ
                start(sibling(slot, hop if way == 0 else NZ - hop))
        for way in range(2):
            if hop <= y_hops[way]:
                y_copy(way, hop - 1).wait_recv()
                if hop < y_hops[way]:
                    start(y_copy(way, hop))
    for n in range(NZ):
        sibling(z, n).wait_recv()
    for c in started:
        c.wait_send()


def offsets(per):
    sizes = (("slot", 4 * NY), ("half", 4 * NY), ("prev1", 8 * NY), ("last1", per), ("prev2", NY * 2 * per), ("last2", NY * per))
    out, at = {}, 0
    for name, size in sizes:
        out[name] = at
        at += size
    return out


def purify(
    per, table, panel, row, keep, keep_out, square, purified, parts, first, second, total, ys, yr
):
    x, z, core, y = place()
    south, north = (y + NY - 1) % NY, (y + 1) % NY
    greet([to(x, z, core, south), to(x, z, core, north)])
    at = offsets(per)
    near = NY // 2

    def hops(h):
        longer, shorter = near, NY - 1 - near
        return (longer, shorter) if h % 2 == 0 else (shorter, longer)

    def y_copy(h, way, hop):
        slot = (y + NY - hop) % NY if way == 0 else (y + hop) % NY
        return copy(
            parts[h].at[slot], ys.at[h, way, hop], yr.at[h, way, hop], to(x, z, core, north if way == 0 else south)
        )

    started = []

    def start(c):
        c.start()
        started.append(c)

    first[8 * NY] = jnp.zeros((CP, TWO), F32)
    second[2 * per] = jnp.zeros((BLK, TWO), F32)
    lanes = lax.broadcasted_iota(I32, (2 * CP, TWO), 1) // BLK
    side = lax.broadcasted_iota(I32, (CP, TWO), 1) // BLK

    def first_part(h):
        def one_panel(q, _):
            high_w, low_w = split(row[q, :TWO])
            wide = jnp.concatenate([high_w, low_w], axis=1)
            stack = []
            for n in range(4):
                e = q * 4 + n
                block = panel[table[at["slot"] + e], 2 * CP * h : 2 * CP * (h + 1), :]
                block = jnp.where(table[at["half"] + e] == n % 2, block, pltpu.roll(block, BLK, 1))
                stack.append(jnp.where(lanes == n % 2, block, 0.0))
            high, low = split(jnp.concatenate(stack, axis=0))
            both = dot(high, wide)
            made = both[:, :TWO] + both[:, TWO:] + dot(low, high_w)
            for n in range(8):
                e = q * 8 + n
                term = jnp.where(side == n // 4, made[n * CP : (n + 1) * CP], 0.0)
                first[e] = term + first[table[at["prev1"] + e]]
            return 0

        lax.fori_loop(0, NY, one_panel, 0)

        def one_column(j, _):
            parts[h][y, j] = first[table[at["last1"] + j]] * keep[j]
            return 0

        lax.fori_loop(0, per, one_column, 0)

    def second_piece(q, fresh):
        def one_device(d, _):
            device = q * (per // 2) + d
            slot = ((device // 2) % NZ * 2 + device % 2) * NX + device // (2 * NZ)
            high, low = split(panel[slot, :TWO, :])
            halves = [
                split(jnp.concatenate([parts[h][q, d * 2 + r] for h in range(NP)], axis=0)) for r in range(2)
            ]
            none = jnp.zeros((BLK, TWO), BF16)
            high_w, low_w = (
                jnp.concatenate(
                    [
                        jnp.concatenate([halves[0][v], none], axis=1),
                        jnp.concatenate([none, halves[1][v]], axis=1),
                    ],
                    axis=0,
                )
                for v in range(2)
            )
            made = dot(jnp.concatenate([high, low], axis=1), jnp.concatenate([high_w, high_w], axis=0))
            made = made + dot(high, low_w)
            for r in range(2):
                for s in range(2):
                    e = d * 4 + r * 2 + s
                    before = second[table[at["prev2"] + q * 2 * per + e]]
                    term = jnp.concatenate(
                        [
                            made[(h * 2 + s) * CP : (h * 2 + s + 1) * CP, r * TWO : (r + 1) * TWO]
                            for h in range(NP)
                        ],
                        axis=0,
                    )
                    second[e] = term + before
            return 0

        lax.fori_loop(0, per // 2, one_device, 0)

        def one_column(j, _):
            new = second[table[at["last2"] + q * per + j]]
            total[j] = new if fresh else total[j] + new
            return 0

        lax.fori_loop(0, per, one_column, 0)

    for h in range(NP):
        first_part(h)
        for way in range(2):
            if hops(h)[way]:
                start(y_copy(h, way, 0))
    second_piece(y, True)

    def own(pair):
        return jnp.concatenate([parts[h][y, pair * 2 + b] for b in range(2) for h in range(NP)], axis=0)

    for pair in range(per // 2):
        square[:, pair * TWO : (pair + 1) * TWO] = own(pair).T

    for hop in range(1, near + 1):
        for h in range(NP):
            for way in range(2):
                if hop <= hops(h)[way]:
                    y_copy(h, way, hop - 1).wait_recv()
                    if hop < hops(h)[way]:
                        start(y_copy(h, way, hop))
        second_piece((y + NY - hop) % NY, False)
        if 2 * hop < NY:
            second_piece((y + hop) % NY, False)
    for pair in range(per // 2):
        cube = jnp.concatenate([total[pair * 2 + b] * keep_out[pair * 2 + b] for b in range(2)], axis=0)
        purified[:, pair * TWO : (pair + 1) * TWO] = (3.0 * own(pair) - 2.0 * cube).T
    for c in started:
        c.wait_send()


def chain(ids, per, none):
    n = ids.shape[-1]
    spot = jnp.arange(n, dtype=I32)
    same = (ids[..., :, None] == ids[..., None, :]) & (spot[None, :] < spot[:, None])
    prev = jnp.max(jnp.where(same, spot, -1), axis=-1)
    here = ids[..., None, :] == jnp.arange(per, dtype=I32)[:, None]
    last = jnp.max(jnp.where(here, spot, -1), axis=-1)
    return jnp.where(prev < 0, none, prev), jnp.where(last < 0, none, last)


def local(values, column_ids, counts, keep_pattern):
    per = keep_pattern.shape[1]
    nb = 2 * lax.axis_size("row")
    vmem, smem = pl.BlockSpec(memory_space=pltpu.VMEM), pl.BlockSpec(memory_space=pltpu.SMEM)
    rows = TWO + EXTRA
    dma = pltpu.SemaphoreType.DMA
    panel, row = pl.pallas_call(
        gather_panel,
        out_shape=(
            jax.ShapeDtypeStruct((NZ, 2, NX, rows, TWO), F32),
            jax.ShapeDtypeStruct((NY, rows, TWO), F32),
        ),
        in_specs=[smem, smem, vmem],
        out_specs=(vmem, vmem),
        scratch_shapes=[
            dma((NX - 1,)), dma((NX - 1,)),
            dma((2, NZ)), dma((2, NZ)),
            dma((NZ,)), dma((NZ,)),
            dma((2, NY)), dma((2, NY)),
        ],
        compiler_params=pltpu.CompilerParams(
            collective_id=0, has_side_effects=True, vmem_limit_bytes=24 << 20
        ),
        name="gather_panel",
    )(column_ids, counts, values)

    tags = panel[:, :, :, TWO, :4].astype(I32)
    ids = tags.transpose(2, 0, 1, 3).reshape(nb, 2)
    mine = row[:, TWO, :4].astype(I32)
    block = (mine + jnp.arange(NY, dtype=I32)[:, None] * per).reshape(-1)
    device = block // 2
    slot = ((device // 2) % NZ * 2 + device % 2) * NX + device // (2 * NZ)
    onto = jnp.sum(
        jnp.where((block[:, None] == jnp.arange(nb, dtype=I32)[None, :])[:, :, None], ids[None], 0), axis=1
    )
    prev1, last1 = chain(onto.reshape(-1), per, 8 * NY)
    prev2, last2 = chain(ids.reshape(NY, 2 * per), per, 2 * per)
    table = jnp.concatenate(
        [slot, block % 2, prev1, last1, prev2.reshape(-1), last2.reshape(-1)]
    ).astype(I32)
    keep = jnp.repeat(keep_pattern.astype(F32).T, BLK, axis=1)[:, None, :]

    def body(table, panel, row, keep, square, purified, *rest):
        parts = rest[:NP]
        purify(per, table, panel, row, keep, keep, square, purified, parts, *rest[NP:])

    square, purified = pl.pallas_call(
        body,
        out_shape=(
            jax.ShapeDtypeStruct((TWO, per * BLK), F32),
            jax.ShapeDtypeStruct((TWO, per * BLK), F32),
        ),
        in_specs=[smem, vmem, vmem, vmem],
        out_specs=(vmem, vmem),
        scratch_shapes=[pltpu.VMEM((NY, per, CP, TWO), F32) for _ in range(NP)]
        + [
            pltpu.VMEM((8 * NY + 1, CP, TWO), F32),
            pltpu.VMEM((2 * per + 1, BLK, TWO), F32),
            pltpu.VMEM((per, BLK, TWO), F32),
            dma((NP, 2, NY)), dma((NP, 2, NY)),
        ],
        compiler_params=pltpu.CompilerParams(
            collective_id=1, has_side_effects=True, vmem_limit_bytes=48 << 20
        ),
        name="purify",
    )(table, panel.reshape(NZ * 2 * NX, rows, TWO), row, keep)
    return square, purified


def solution(mesh):
    return jax.shard_map(
        local,
        mesh=mesh,
        in_specs=(P("row", "col"), P("row", "col"), P("row", "col"), P("row", "col")),
        out_specs=(P("row", "col"), P("row", "col")),
        check_vma=False,
    )
```

time: 523 us -> 154 us (0.29)
  blocking collectives: 313 us -> 0 us
  Pallas kernels: 0 us -> 142 us
  matrix products: 70.9 us -> 0 us
  waiting for transfers between devices: 69.9 us -> 0 us
  local copies, waits for them, and re-layouts: 49.6 us -> 8.05 us
  between operations: 15.5 us -> 0.75 us
    all_gather x4 -> x0, blocking collectives: 301 us -> none  [the longest x1 185 us: local(): lax.all_gather(live_counts, 'row', axis=0, tiled=True)]
    pallas_call x0 -> x2, Pallas kernels: none -> 142 us  [the longest x1 72.3 us: local(): pl.pallas_call(body, out_shape=(jax.ShapeDtypeStruct((TWO, per * BLK), F3...]
    dot_general x25 -> x0, matrix products: 70.9 us -> none  [the longest x12 38.5 us: add_group(): jnp.einsum('akb,kbsc->ksac', left_part, blocks, precision=lax.Precision.H...]
    all_gather x2 -> x0, waiting for transfers between devices: 69.2 us -> none  [the longest x1 69.2 us: local(): square_row = lax.all_gather(square, 'col', axis=1, tiled=True)]
    dynamic_slice x36 -> x0, local copies, waits for them, and re-layouts: 22.6 us -> none  [the longest x12 20.8 us: add_group(): group_tiles = lax.dynamic_slice_in_dim(tiles, offset, group_rows, 0)]
    unnamed x16 -> x9, local copies, waits for them, and re-layouts: 25.8 us -> 6.78 us
    unnamed x1 -> x0, blocking collectives: 12 us -> none
  transfers between devices with their start and end apart: 2 -> 0, of which waited for: 1 -> 0; matrix products, arithmetic and copies ran while one was open for 4% -> 0% of each run, Pallas kernels for 0% -> 0%
where the time goes in v1:
time: 154 us; the launch traced here: 153 us
  Pallas kernels  142 us (92%)
  local copies, waits for them, and re-layouts  8.05 us (5%)
  other arithmetic  2.83 us (2%)
    pallas_call x1, Pallas kernels, local(): pl.pallas_call(body, out_shape=(jax.ShapeDtypeStruct((TWO, per * BLK), F3...  72.3 us
    pallas_call x1, Pallas kernels, local(): pl.pallas_call(gather_panel, out_shape=(jax.ShapeDtypeStruct((NZ, 2, NX,...  69.3 us
    unnamed x9, local copies, waits for them, and re-layouts  6.78 us

profile of v1, /device:TPU:1, one launch (start us, length us, event | category | flops | bytes accessed | tf_op | source)
XLA Modules:
  0.0 153.2 jit_solution(594255393624545782)
XLA Ops:
  0.6 0.7 copy.12.counts
  1.4 0.7 convert_bitcast_fusion
  2.1 0.1 add.38
  2.1 0.1 add.39
  2.2 0.1 copy.17
  2.3 0.1 broadcast_in_dim.98
  2.4 0.1 broadcast_in_dim_reshape.2.keep
  2.5 0.0 copy-start.1
  2.5 0.8 copy-done.1
  3.3 0.0 copy-start.2
  3.3 0.7 copy-done.2
  4.0 69.3 %gather_panel.1 = (f32[12,2,4,136,128]{4,3,2,1,0:T(8,128)S(1)}, f32[8,136,128]{2,1,0:T(8,128)S(1)}) custom-call(s32[2,2]{1,0:T(2,128)S(1)} %copy-done.2, s32[2,1]{1,0:T(2,128)S(1)} %copy.12.counts, f32[128,128]{1,0:T(8,128)S(1)} %copy-done.1), custom_call_target="tpu_custom_call" | custom-call | tf_op jit(solution)/shard_map/gather_panel/pallas_call | solution.py:284
  73.4 0.0 copy-start
  73.4 2.8 %copy-done = f32[12,2,4,136,128]{4,3,2,1,0:T(8,128)} copy-done((f32[12,2,4,136,128]{4,3,2,1,0:T(8,128)}, f32[12,2,4,136,128]{4,3,2,1,0:T(8,128)S(1)}, u32[]{:S(2)}) %copy-start) | copy-done | bytes 6684696
  76.1 0.1 convert_element_type.21
  76.3 0.1 iota_compare_fusion.2
  76.3 1.0 slice_convert_fusion
  77.4 0.1 eq.87
  77.5 0.3 select_reduce_fusion
  77.8 0.1 reduce_max.43
  77.9 0.2 select_reduce_fusion.1
  78.1 0.1 reduce_max.45
  78.2 0.1 broadcast_in_dim.83
  78.4 0.1 copy.14
  78.4 0.1 select_reduce_fusion.2
  78.6 0.1 copy.15
  78.6 0.1 eq.80
  78.8 0.2 select_reduce_fusion.3
  78.9 0.1 select_reduce_fusion.4
  79.1 0.1 concatenate.3.table
  79.2 72.3 %purify.1 = (f32[128,1536]{1,0:T(8,128)S(1)}, f32[128,1536]{1,0:T(8,128)S(1)}) custom-call(s32[728]{0:T(1024)S(1)} %concatenate.3.table, f32[96,136,128]{2,1,0:T(8,128)} %bitcast.6, f32[8,136,128]{2,1,0:T(8,128)S(1)} %get-tuple-element.4.row, f32[24,1,128]{2,1,0:T(1,128)S(1)} %broadcast_in_dim_reshape.2.keep), custom_call_target="tpu_custom_call" | custom-call | tf_op jit(solution)/shard_map/purify/pallas_call | solution.py:324
  151.5 0.9 copy.20
  152.3 0.9 copy.21
  (10 shorter events, 0.1 us)
Async XLA Ops:
  2.5 0.8 copy-start.1
  3.3 0.7 copy-start.2
  73.4 2.8 %copy-start = (f32[12,2,4,136,128]{4,3,2,1,0:T(8,128)}, f32[12,2,4,136,128]{4,3,2,1,0:T(8,128)S(1)}, u32[]{:S(2)}) copy-start(f32[12,2,4,136,128]{4,3,2,1,0:T(8,128)S(1)} %get-tuple-element.5) | copy-start | bytes 20054020

commit v2 on v0

v2 whole, which is shorter than its diff:
```python
import jax
import jax.numpy as jnp
from jax import lax
from jax.experimental import pallas as pl
from jax.experimental.pallas import tpu as pltpu
from jax.sharding import PartitionSpec as P

MESH = pl.DeviceIdType.MESH
NX, NZ, NY = 4, 12, 8
BLK = 64
TWO = 2 * BLK
NP = 4
AHEAD = 2
CP = BLK // NP
EXTRA = 8
F32, BF16, I32 = jnp.float32, jnp.bfloat16, jnp.int32


def place():
    row, col = lax.axis_index("row"), lax.axis_index("col")
    return row // (2 * NZ), (row // 2) % NZ, row % 2, col


def to(x, z, core, y):
    return ((x * NZ + z) * 2 + core, y)


def greet(partners):
    barrier = pltpu.get_barrier_semaphore()
    for partner in partners:
        pl.semaphore_signal(barrier, inc=1, device_id=partner, device_id_type=MESH)
    pl.semaphore_wait(barrier, len(partners))


def send(src, dst, sems, at, target):
    return pltpu.make_async_remote_copy(
        src_ref=src, dst_ref=dst, send_sem=sems[0].at[at], recv_sem=sems[1].at[at], device_id=target, device_id_type=MESH
    )


def split(a):
    high = a.astype(BF16)
    return high, (a - high.astype(F32)).astype(BF16)


def dot(a, b):
    return jnp.dot(a, b, preferred_element_type=F32)


def part_rows(h):
    return 2 * CP + (EXTRA if h == 0 else 0)


def iota(shape, axis):
    return lax.broadcasted_iota(I32, shape, axis)


def over(a, size, count):
    return sum(((a >= size * n).astype(I32) for n in range(1, count)), jnp.zeros(a.shape, I32))


def make_tables(tags, mine, per):
    ndev = tags.shape[0]
    each = per // 2
    bits = NY.bit_length() - 1
    tags, mine = (jnp.clip(a.astype(I32), 0, per - 1) for a in (tags, mine))
    sub, lane = iota((ndev, TWO), 0), iota((ndev, TWO), 1)
    piece_s, piece_l = over(sub, each, NY), over(lane, each, NY + 1)
    ids = [jnp.broadcast_to(tags[:, n : n + 1], (ndev, TWO)) for n in range(4)]
    rank_s = [(sub - each * piece_s) * 4 + n for n in range(4)]

    def top(terms, none):
        best = None
        for mask, rank in terms:
            new = jnp.where(mask, rank, -1)
            best = new if best is None else jnp.maximum(best, new)
        best = jnp.max(best, axis=0, keepdims=True)
        return jnp.where(best < 0, none, best)

    lane1, sub1 = iota((NY, TWO), 1), iota((NY, TWO), 0)
    block = jnp.zeros((NY, TWO), I32)
    for n in range(4):
        hit = ((lane1 >> bits) == n) & ((lane1 & (NY - 1)) == sub1)
        block = block + jnp.where(hit, jnp.broadcast_to(mine[:, n : n + 1], (NY, TWO)), 0)
    block = jnp.sum(block, axis=0, keepdims=True)
    lane0 = iota((1, TWO), 1)
    half = block & 1
    device = (lane0 & (NY - 1)) * each + (block >> 1)
    onto = []
    for s in range(2):
        chosen = jnp.where(half == 0, ids[s], ids[2 + s])
        onto.append(jnp.sum(jnp.where(sub == device, chosen, 0), axis=0, keepdims=True))
    count = 4 * NY
    sub2, lane2 = iota((count, TWO), 0), iota((count, TWO), 1)
    onto_s = [
        jnp.broadcast_to(jnp.sum(jnp.where(sub2 == lane2, onto[s], 0), axis=1, keepdims=True), (count, TWO))
        for s in range(2)
    ]

    def rank1(a, s):
        return ((a & (NY - 1)) * 4 + (a >> bits)) * 2 + s

    rows = [device, half]
    for s in range(2):
        rows.append(
            top(
                (((onto_s[t] == onto[s]) & (rank1(sub2, t) < rank1(lane2, s)), rank1(sub2, t)) for t in range(2)), 8 * NY
            )
        )
    rows.append(top(((onto_s[t] == lane2, rank1(sub2, t)) for t in range(2)), 8 * NY))
    for n in range(4):
        own = jnp.sum(jnp.where(sub == lane, ids[n], 0), axis=0, keepdims=True)
        rank_l = (lane - each * piece_l) * 4 + n
        rows.append(
            top(
                (((piece_s == piece_l) & (ids[m] == own) & (rank_s[m] < rank_l), rank_s[m]) for m in range(4)), 2 * per
            )
        )
    for g in range(-(-NY * per // TWO)):
        where = lane + g * TWO
        q = over(where, per, NY + 1)
        column = where - per * q
        rows.append(top((((piece_s == q) & (ids[m] == column), rank_s[m]) for m in range(4)), 2 * per))
    return rows + [jnp.zeros((1, TWO), I32)] * (TABLE - len(rows))


DEVICE, HALF, PREV1, LAST1, PREV2, LAST2, TABLE = 0, 1, 2, 4, 5, 9, 16


def purify(
    per, ids, counts, tile, keep_pattern, square, purified,
    panel, parts, row, early, late, first, second, total, keep, tags, table_v, table,
    z_sems, r_sems, x_sems, s_sems, y_sems, own_sem, table_sem,
):
    x, z, core, y = place()
    west, east = (z + NZ - 1) % NZ, (z + 1) % NZ
    south, north = (y + NY - 1) % NY, (y + 1) % NY
    before, after = (x + NX - 1) % NX, (x + 1) % NX
    twin = to(x, z, 1 - core, y)
    near = NY // 2
    z_hops = (NZ // 2, NZ - 1 - NZ // 2)
    r_hops = (near, NY - 1 - near)

    def y_hops(h):
        return r_hops if h % 2 == 0 else r_hops[::-1]

    started = []

    def start(c):
        c.start()
        started.append(c)

    def z_copy(g, way, hop):
        ref = (early, late)[g]
        slot = (z + NZ - hop) % NZ if way == 0 else (z + hop) % NZ
        return send(ref.at[slot], ref.at[slot], z_sems, (g, way, hop), to(x, east if way == 0 else west, core, y))

    def z_step(g, hop):
        for way in range(2):
            if 1 <= hop <= z_hops[way]:
                z_copy(g, way, hop - 1).wait_recv()
            if hop < z_hops[way]:
                start(z_copy(g, way, hop))

    def ring_y(ref, sems, at, way, hop):
        slot = (y + NY - hop) % NY if way == 0 else (y + hop) % NY
        return send(ref.at[slot], ref.at[slot], sems, at + (way, hop), to(x, z, core, north if way == 0 else south))

    def r_step(hop):
        for way in range(2):
            if 1 <= hop <= r_hops[way]:
                ring_y(row, r_sems, (), way, hop - 1).wait_recv()
            if hop < r_hops[way]:
                start(ring_y(row, r_sems, (), way, hop))

    def y_step(h, hop):
        for way in range(2):
            if 1 <= hop <= y_hops(h)[way]:
                ring_y(parts[h], y_sems, (h,), way, hop - 1).wait_recv()
            if hop < y_hops(h)[way]:
                start(ring_y(parts[h], y_sems, (h,), way, hop))

    def slab(h, at):
        return panel[h].at[pl.ds(at * NZ, NZ), core]

    def source(h):
        ref, at = (early, 2 * CP * h + (EXTRA if h else 0)) if h < AHEAD else (late, 2 * CP * (h - AHEAD))
        return ref.at[:, at : at + part_rows(h)]

    def x_copy(h, n):
        if n == 0:
            return send(source(h), slab(h, x), x_sems, (h, 0), to(after, z, core, y))
        if n == 1:
            return send(source(h), slab(h, x), x_sems, (h, 1), to(before, z, core, y))
        held = slab(h, jnp.where(core == 0, before, after))
        return send(held, held, x_sems, (h, 2), to(jnp.where(core == 0, after, before), z, core, y))

    def own_copy(h):
        return pltpu.make_async_copy(source(h), slab(h, x), own_sem.at[h])

    def s_copy(h, n):
        if n == 0:
            return send(source(h), slab(h, x), s_sems, (h, 0), twin)
        held = slab(h, (before, after, (x + 2) % NX)[n - 1])
        return send(held, held, s_sems, (h, n), twin)

    def x_begin(h):
        for n in range(2):
            start(x_copy(h, n))
        own_copy(h).start()
        start(s_copy(h, 0))

    def x_middle(h):
        for n in range(2):
            x_copy(h, n).wait_recv()
        start(x_copy(h, 2))
        for n in range(1, 3):
            start(s_copy(h, n))

    def x_end(h):
        x_copy(h, 2).wait_recv()
        start(s_copy(h, 3))
        own_copy(h).wait()
        for n in range(4):
            s_copy(h, n).wait_recv()

    greet(
        [to(after, z, core, y), to(before, z, core, y), to(x, west, core, y), to(x, east, core, y)]
        + [twin, to(x, z, core, south), to(x, z, core, north)]
    )

    at_row, at_lane = iota((TWO, TWO), 0), iota((TWO, TWO), 1)
    live = jnp.where(at_row < BLK, counts[0:1, 0:1], counts[1:2, 0:1])
    held = jnp.where((at_lane >= BLK).astype(I32) < live, tile[...], 0.0).T
    lane = iota((EXTRA, TWO), 1)
    mark = jnp.where(
        lane == 0,
        ids[0:1, 0:1],
        jnp.where(lane == 1, ids[0:1, 1:2], jnp.where(lane == 2, ids[1:2, 0:1], ids[1:2, 1:2])),
    ).astype(F32)
    row[y, :TWO] = held
    row[y, TWO:] = mark
    for h in range(NP):
        ref, at = (early, 2 * CP * h + (EXTRA if h else 0)) if h < AHEAD else (late, 2 * CP * (h - AHEAD))
        for s in range(2):
            ref[z, at + s * CP : at + (s + 1) * CP] = held[s * BLK + h * CP : s * BLK + (h + 1) * CP]
    early[z, 2 * CP : 2 * CP + EXTRA] = mark
    z_step(0, 0)
    r_step(0)

    first[8 * NY] = jnp.zeros((CP, TWO), F32)
    second[2 * per] = jnp.zeros((BLK, TWO), F32)
    square_iota = iota((per, per), 0) == iota((per, per), 1)
    keeps = [
        jnp.sum(jnp.where(square_iota, keep_pattern[r : r + 1, :], 0).astype(F32), axis=1, keepdims=True) for r in range(2)
    ]
    keep[...] = jnp.where(iota((per, TWO), 1) < BLK, keeps[0], keeps[1])

    for hop in range(1, max(NZ // 2, near) + 1):
        z_step(0, hop)
        r_step(hop)
    for h in range(AHEAD):
        x_begin(h)
    for hop in range(4):
        z_step(1, hop)
    x_middle(0)
    z_step(1, 4)
    z_step(1, 5)
    x_end(0)
    for hop in range(6, NZ // 2 + 1):
        z_step(1, hop)
    for h in range(AHEAD, NP):
        x_begin(h)

    def tag_row(n, _):
        for c in range(2):
            tags[pl.ds(2 * n + c, 1), :] = panel[0][n, c, 2 * CP : 2 * CP + 1, :]
        return 0

    lax.fori_loop(0, NX * NZ, tag_row, 0)
    mine = jnp.concatenate([row[q, TWO : TWO + 1, :] for q in range(NY)], axis=0)
    for n, line in enumerate(make_tables(tags[...], mine, per)):
        table_v[n : n + 1, :] = line
    fetch = pltpu.make_async_copy(table_v, table, table_sem)
    fetch.start()
    fetch.wait()

    bits = NY.bit_length() - 1
    lanes = iota((2 * CP, TWO), 1) // BLK
    side = iota((CP, TWO), 1) // BLK

    def first_part(h):
        def one_panel(q, _):
            high_w, low_w = split(row[q, :TWO])
            wide = jnp.concatenate([high_w, low_w], axis=1)
            stack = []
            for n in range(4):
                e = (n << bits) + q
                device = table[DEVICE, e]
                block = panel[h][device // 2, device % 2, : 2 * CP, :]
                block = jnp.where(table[HALF, e] == n % 2, block, pltpu.roll(block, BLK, 1))
                stack.append(jnp.where(lanes == n % 2, block, 0.0))
            high, low = split(jnp.concatenate(stack, axis=0))
            both = dot(high, wide)
            made = both[:, :TWO] + both[:, TWO:] + dot(low, high_w)
            for n in range(8):
                term = jnp.where(side == n // 4, made[n * CP : (n + 1) * CP], 0.0)
                first[q * 8 + n] = term + first[table[PREV1 + n % 2, ((n // 2) << bits) + q]]
            return 0

        lax.fori_loop(0, NY, one_panel, 0)

        def one_column(j, _):
            parts[h][y, j] = first[table[LAST1, j]] * keep[pl.ds(j, 1), :]
            return 0

        lax.fori_loop(0, per, one_column, 0)

    quarter = BLK // 2

    def half_pass(q, half, fresh):
        here = range(half * NP // 2, (half + 1) * NP // 2)
        inside = (iota((TWO, TWO), 1) % BLK) // quarter == half

        def one_device(d, _):
            device = q * (per // 2) + d
            block = jnp.concatenate([panel[h][device // 2, device % 2, : 2 * CP, :] for h in range(NP)], axis=0)
            high = block.astype(BF16)
            rough = high.astype(F32)
            rest = pltpu.roll(block - rough, quarter if half == 0 else TWO - quarter, 1)
            mixed = jnp.where(inside, rough, rest).astype(BF16)
            none = jnp.zeros((BLK, TWO), BF16)
            blank = jnp.zeros((quarter, TWO), BF16)
            upper, lower = [], []
            for r in range(2):
                high_w, low_w = split(jnp.concatenate([parts[h][q, d * 2 + r] for h in here], axis=0))
                twice = jnp.concatenate([high_w, high_w], axis=0)
                once = jnp.concatenate([low_w, blank] if half == 0 else [blank, low_w], axis=0)
                upper.append(jnp.concatenate([twice, none] if r == 0 else [none, twice], axis=1))
                lower.append(jnp.concatenate([once, none] if r == 0 else [none, once], axis=1))
            made = dot(jnp.concatenate([mixed, high], axis=1), jnp.concatenate(upper + lower, axis=0))
            for r in range(2):
                for s in range(2):
                    term = jnp.concatenate(
                        [made[(h * 2 + s) * CP : (h * 2 + s + 1) * CP, r * TWO : (r + 1) * TWO] for h in range(NP)],
                        axis=0,
                    )
                    second[d * 4 + r * 2 + s] = term + second[table[PREV2 + r * 2 + s, device]]
            return 0

        lax.fori_loop(0, per // 2, one_device, 0)

        def one_column(j, _):
            at = q * per + j
            new = second[table[LAST2 + at // TWO, at % TWO]]
            total[j] = new if fresh else total[j] + new
            return 0

        lax.fori_loop(0, per, one_column, 0)

    def own(pair):
        return jnp.concatenate([parts[h][y, pair * 2 + b] for b in range(2) for h in range(NP)], axis=0)

    def arrived(hop, half):
        half_pass((y + NY - hop) % NY, half, False)
        if 2 * hop < NY:
            half_pass((y + hop) % NY, half, False)

    for tick in range(NP + near):
        if 1 <= tick < NP:
            x_end(tick)
        if tick < NP:
            first_part(tick)
            y_step(tick, 0)
        if tick + 1 < NP:
            x_middle(tick + 1)
        for hop in range(1, near + 1):
            if 0 <= tick - hop < NP:
                y_step(tick - hop, hop)
        if tick == NP - 1:
            half_pass(y, 0, True)
            arrived(1, 0)
        if NP <= tick <= NP + near - 2:
            arrived(tick - NP + 2, 0)
        if tick == NP:
            half_pass(y, 1, False)
            for pair in range(per // 2):
                square[:, pair * TWO : (pair + 1) * TWO] = own(pair).T
        if tick >= NP:
            arrived(tick - NP + 1, 1)
    for pair in range(per // 2):
        cube = jnp.concatenate(
            [total[pair * 2 + b] * keep[pair * 2 + b : pair * 2 + b + 1, :] for b in range(2)], axis=0
        )
        purified[:, pair * TWO : (pair + 1) * TWO] = (3.0 * own(pair) - 2.0 * cube).T
    for c in started:
        c.wait_send()


def local(values, column_ids, counts, keep_pattern):
    per = keep_pattern.shape[1]
    ndev = NX * NZ * 2
    vmem = pl.BlockSpec(memory_space=pltpu.VMEM)

    def dma(*shape):
        return [pltpu.SemaphoreType.DMA(shape), pltpu.SemaphoreType.DMA(shape)]

    def body(ids, counts, tile, keep_pattern, square, purified, *rest):
        panel, parts, others, sems = rest[:NP], rest[NP : 2 * NP], rest[2 * NP : 2 * NP + 10], rest[2 * NP + 10 :]
        pairs = [sems[2 * n : 2 * n + 2] for n in range(5)]
        purify(
            per, ids, counts, tile, keep_pattern, square, purified, panel, parts, *others, *pairs, sems[10], sems[11]
        )

    out = jax.ShapeDtypeStruct((TWO, per * BLK), F32)
    return pl.pallas_call(
        body,
        out_shape=(out, out),
        in_specs=[vmem] * 4,
        out_specs=(vmem, vmem),
        scratch_shapes=[pltpu.VMEM((NX * NZ, 2, part_rows(h), TWO), F32) for h in range(NP)]
        + [pltpu.VMEM((NY, per, CP, TWO), F32) for _ in range(NP)]
        + [
            pltpu.VMEM((NY, TWO + EXTRA, TWO), F32),
            pltpu.VMEM((NZ, 2 * CP * AHEAD + EXTRA, TWO), F32),
            pltpu.VMEM((NZ, 2 * CP * (NP - AHEAD), TWO), F32),
            pltpu.VMEM((8 * NY + 1, CP, TWO), F32),
            pltpu.VMEM((2 * per + 1, BLK, TWO), F32),
            pltpu.VMEM((per, BLK, TWO), F32),
            pltpu.VMEM((per, TWO), F32),
            pltpu.VMEM((ndev, TWO), F32),
            pltpu.VMEM((TABLE, TWO), I32),
            pltpu.SMEM((TABLE, TWO), I32),
        ]
        + dma(2, 2, NZ) + dma(2, NY) + dma(NP, 3) + dma(NP, 4) + dma(NP, 2, NY)
        + [pltpu.SemaphoreType.DMA((NP,)), pltpu.SemaphoreType.DMA],
        compiler_params=pltpu.CompilerParams(collective_id=0, has_side_effects=True, vmem_limit_bytes=48 << 20),
        name="purify",
    )(column_ids, counts, values, keep_pattern)


def solution(mesh):
    return jax.shard_map(
        local,
        mesh=mesh,
        in_specs=(P("row", "col"), P("row", "col"), P("row", "col"), P("row", "col")),
        out_specs=(P("row", "col"), P("row", "col")),
        check_vma=False,
    )
```

time: 523 us -> 160 us (0.31)
  blocking collectives: 313 us -> 0 us
  Pallas kernels: 0 us -> 155 us
  matrix products: 70.9 us -> 0 us
  waiting for transfers between devices: 69.9 us -> 0 us
  local copies, waits for them, and re-layouts: 49.6 us -> 4.03 us
  between operations: 15.5 us -> 0.65 us
    all_gather x4 -> x0, blocking collectives: 301 us -> none  [the longest x1 185 us: local(): lax.all_gather(live_counts, 'row', axis=0, tiled=True)]
    pallas_call x0 -> x1, Pallas kernels: none -> 155 us  [local(): pl.pallas_call(body, out_shape=(out, out), in_specs=[vmem] * 4, out_specs...]
    dot_general x25 -> x0, matrix products: 70.9 us -> none  [the longest x12 38.5 us: add_group(): jnp.einsum('akb,kbsc->ksac', left_part, blocks, precision=lax.Precision.H...]
    all_gather x2 -> x0, waiting for transfers between devices: 69.2 us -> none  [the longest x1 69.2 us: local(): square_row = lax.all_gather(square, 'col', axis=1, tiled=True)]
    dynamic_slice x36 -> x0, local copies, waits for them, and re-layouts: 22.6 us -> none  [the longest x12 20.8 us: add_group(): group_tiles = lax.dynamic_slice_in_dim(tiles, offset, group_rows, 0)]
    unnamed x16 -> x9, local copies, waits for them, and re-layouts: 25.8 us -> 4.03 us
    unnamed x1 -> x0, blocking collectives: 12 us -> none
  transfers between devices with their start and end apart: 2 -> 0, of which waited for: 1 -> 0; matrix products, arithmetic and copies ran while one was open for 4% -> 0% of each run, Pallas kernels for 0% -> 0%
where the time goes in v2:
time: 160 us
  Pallas kernels  155 us (97%)
  local copies, waits for them, and re-layouts  4.03 us (3%)
    pallas_call x1, Pallas kernels, local(): pl.pallas_call(body, out_shape=(out, out), in_specs=[vmem] * 4, out_specs...  155 us
    unnamed x9, local copies, waits for them, and re-layouts  4.03 us

profile of v2, /device:TPU:1, one launch (start us, length us, event | category | flops | bytes accessed | tf_op | source)
XLA Modules:
  0.0 159.6 jit_solution(15016623143272225117)
XLA Ops:
  0.6 0.0 copy-start.1
  0.6 0.7 copy.6.counts
  1.4 0.0 copy-done.1
  1.4 0.0 copy-start
  1.4 0.8 copy-done
  2.2 0.0 copy-start.2
  2.2 0.7 copy-done.2
  2.9 154.9 %purify.1 = (f32[128,1536]{1,0:T(8,128)S(1)}, f32[128,1536]{1,0:T(8,128)S(1)}) custom-call(s32[2,2]{1,0:T(2,128)S(1)} %copy-done.1, s32[2,1]{1,0:T(2,128)S(1)} %copy.6.counts, f32[128,128]{1,0:T(8,128)S(1)} %copy-done, s32[2,24]{1,0:T(2,128)S(1)} %copy-done.2), custom_call_target="tpu_custom_call" | custom-call | tf_op jit(solution)/shard_map/purify/pallas_call | solution.py:416
  157.8 0.9 copy.9
  158.7 0.9 copy.10
Async XLA Ops:
  0.6 0.8 copy-start.1
  1.4 0.8 copy-start
  2.2 0.7 copy-start.2

commit v3 on v2

--- a/solution.py
+++ b/solution.py
@@ -9,9 +9,12 @@
 NX, NZ, NY = 4, 12, 8
 BLK = 64
 TWO = 2 * BLK
-NP = 4
+WIDTHS = (16, 16, 16, 16)
+LONGER = (0, 1, 0, 1)
+NP = len(WIDTHS)
+AT = tuple(sum(WIDTHS[:h]) for h in range(NP))
 AHEAD = 2
-CP = BLK // NP
+ROWS = tuple(2 * AT[h] - (2 * AT[AHEAD] if h >= AHEAD else 2 * AT[h]) for h in range(NP))
 EXTRA = 8
 F32, BF16, I32 = jnp.float32, jnp.bfloat16, jnp.int32
 
@@ -48,7 +51,7 @@
 
 
 def part_rows(h):
-    return 2 * CP + (EXTRA if h == 0 else 0)
+    return 2 * WIDTHS[h] + (EXTRA if h == 0 else 0)
 
 
 def iota(shape, axis):
@@ -100,7 +103,9 @@
     def rank1(a, s):
         return ((a & (NY - 1)) * 4 + (a >> bits)) * 2 + s
 
-    rows = [device, half]
+    along_x = over(device, 2 * NZ, NX)
+    along_z = (device - 2 * NZ * along_x) >> 1
+    rows = [along_x, half]
     for s in range(2):
         rows.append(
             top(
@@ -121,16 +126,18 @@
         q = over(where, per, NY + 1)
         column = where - per * q
         rows.append(top((((piece_s == q) & (ids[m] == column), rank_s[m]) for m in range(4)), 2 * per))
-    return rows + [jnp.zeros((1, TWO), I32)] * (TABLE - len(rows))
-
-
-DEVICE, HALF, PREV1, LAST1, PREV2, LAST2, TABLE = 0, 1, 2, 4, 5, 9, 16
+    blank = jnp.zeros((1, TWO), I32)
+    rows = rows + [blank] * (ZS - len(rows)) + [along_z, device & 1]
+    return rows + [blank] * (TABLE - len(rows))
+
+
+XS, HALF, PREV1, LAST1, PREV2, LAST2, ZS, CORES, TABLE = 0, 1, 2, 4, 5, 9, 11, 12, 16
 
 
 def purify(
     per, ids, counts, tile, keep_pattern, square, purified,
-    panel, parts, row, early, late, first, second, total, keep, tags, table_v, table,
-    z_sems, r_sems, x_sems, s_sems, y_sems, own_sem, table_sem,
+    panel, parts, row, early, first, second, total, keep, tags, table_v, table,
+    z_sems, r_sems, x_sems, s_sems, y_sems, w_sems, t_sems, own_sem, table_sem,
 ):
     x, z, core, y = place()
     west, east = (z + NZ - 1) % NZ, (z + 1) % NZ
@@ -138,11 +145,12 @@
     before, after = (x + NX - 1) % NX, (x + 1) % NX
     twin = to(x, z, 1 - core, y)
     near = NY // 2
+    wide = panel[AHEAD]
     z_hops = (NZ // 2, NZ - 1 - NZ // 2)
     r_hops = (near, NY - 1 - near)
 
     def y_hops(h):
-        return r_hops if h % 2 == 0 else r_hops[::-1]
+        return r_hops if LONGER[h] == 0 else r_hops[::-1]
 
     started = []
 
@@ -151,9 +159,9 @@
         started.append(c)
 
     def z_copy(g, way, hop):
-        ref = (early, late)[g]
         slot = (z + NZ - hop) % NZ if way == 0 else (z + hop) % NZ
-        return send(ref.at[slot], ref.at[slot], z_sems, (g, way, hop), to(x, east if way == 0 else west, core, y))
+        ref = early.at[slot] if g == 0 else wide.at[:, slot, core]
+        return send(ref, ref, z_sems, (g, way, hop), to(x, east if way == 0 else west, core, y))
 
     def z_step(g, hop):
         for way in range(2):
@@ -181,11 +189,11 @@
                 start(ring_y(parts[h], y_sems, (h,), way, hop))
 
     def slab(h, at):
-        return panel[h].at[pl.ds(at * NZ, NZ), core]
+        return panel[h].at[at, :, core]
 
     def source(h):
-        ref, at = (early, 2 * CP * h + (EXTRA if h else 0)) if h < AHEAD else (late, 2 * CP * (h - AHEAD))
-        return ref.at[:, at : at + part_rows(h)]
+        at = sum(part_rows(g) for g in range(h))
+        return early.at[:, at : at + part_rows(h)]
 
     def x_copy(h, n):
         if n == 0:
@@ -223,6 +231,26 @@
         own_copy(h).wait()
         for n in range(4):
             s_copy(h, n).wait_recv()
+
+    def w_copy(n):
+        at = (x, x, jnp.where(core == 0, before, after))[n]
+        target = (after, before, jnp.where(core == 0, after, before))[n]
+        return send(wide.at[at, z, core], wide.at[at, z, core], w_sems, (n,), to(target, z, core, y))
+
+    def t_copy(n, slot):
+        return send(wide.at[:, slot, core], wide.at[:, slot, core], t_sems, (n,), twin)
+
+    def w_step(hop):
+        z_step(1, hop)
+        if hop == 0:
+            start(t_copy(0, z))
+        for way in range(2):
+            if 1 <= hop <= z_hops[way]:
+                start(t_copy(hop, (z + NZ - hop) % NZ) if way == 0 else t_copy(NZ - hop, (z + hop) % NZ))
+
+    def w_end():
+        for n in range(NZ):
+            t_copy(n, z).wait_recv()
 
     greet(
         [to(after, z, core, y), to(before, z, core, y), to(x, west, core, y), to(x, east, core, y)]
@@ -241,14 +269,21 @@
     row[y, :TWO] = held
     row[y, TWO:] = mark
     for h in range(NP):
-        ref, at = (early, 2 * CP * h + (EXTRA if h else 0)) if h < AHEAD else (late, 2 * CP * (h - AHEAD))
         for s in range(2):
-            ref[z, at + s * CP : at + (s + 1) * CP] = held[s * BLK + h * CP : s * BLK + (h + 1) * CP]
-    early[z, 2 * CP : 2 * CP + EXTRA] = mark
+            chunk = held[s * BLK + AT[h] : s * BLK + AT[h] + WIDTHS[h]]
+            if h < AHEAD:
+                at = sum(part_rows(g) for g in range(h)) + s * WIDTHS[h]
+                early[z, at : at + WIDTHS[h]] = chunk
+            else:
+                at = ROWS[h] + s * WIDTHS[h]
+                wide[x, z, core, at : at + WIDTHS[h]] = chunk
+    early[z, 2 * WIDTHS[0] : 2 * WIDTHS[0] + EXTRA] = mark
     z_step(0, 0)
     r_step(0)
-
-    first[8 * NY] = jnp.zeros((CP, TWO), F32)
+    for n in range(2):
+        start(w_copy(n))
+
+    first[8 * NY] = jnp.zeros((max(WIDTHS), TWO), F32)
     second[2 * per] = jnp.zeros((BLK, TWO), F32)
     square_iota = iota((per, per), 0) == iota((per, per), 1)
     keeps = [
@@ -259,22 +294,25 @@
     for hop in range(1, max(NZ // 2, near) + 1):
         z_step(0, hop)
         r_step(hop)
-    for h in range(AHEAD):
-        x_begin(h)
-    for hop in range(4):
-        z_step(1, hop)
+        if hop == 1:
+            for n in range(2):
+                w_copy(n).wait_recv()
+            start(w_copy(2))
+        if hop == 2:
+            w_copy(2).wait_recv()
+            w_step(0)
+        if hop in (4, 5):
+            w_step(hop - 3)
+    x_begin(0)
+    w_step(3)
     x_middle(0)
-    z_step(1, 4)
-    z_step(1, 5)
+    x_begin(1)
+    w_step(4)
     x_end(0)
-    for hop in range(6, NZ // 2 + 1):
-        z_step(1, hop)
-    for h in range(AHEAD, NP):
-        x_begin(h)
 
     def tag_row(n, _):
         for c in range(2):
-            tags[pl.ds(2 * n + c, 1), :] = panel[0][n, c, 2 * CP : 2 * CP + 1, :]
+            tags[pl.ds(2 * n + c, 1), :] = panel[0][n // NZ, n % NZ, c, 2 * WIDTHS[0] : 2 * WIDTHS[0] + 1, :]
         return 0
 
     lax.fori_loop(0, NX * NZ, tag_row, 0)
@@ -286,63 +324,60 @@
     fetch.wait()
 
     bits = NY.bit_length() - 1
-    lanes = iota((2 * CP, TWO), 1) // BLK
-    side = iota((CP, TWO), 1) // BLK
+
+    def block_of(h, along_x, along_z, side):
+        return panel[min(h, AHEAD)][along_x, along_z, side, ROWS[h] : ROWS[h] + 2 * WIDTHS[h], :]
 
     def first_part(h):
+        cp = WIDTHS[h]
+        lanes = iota((2 * cp, TWO), 1) // BLK
+        side = iota((cp, TWO), 1) // BLK
+
         def one_panel(q, _):
             high_w, low_w = split(row[q, :TWO])
             wide = jnp.concatenate([high_w, low_w], axis=1)
             stack = []
             for n in range(4):
                 e = (n << bits) + q
-                device = table[DEVICE, e]
-                block = panel[h][device // 2, device % 2, : 2 * CP, :]
+                block = block_of(h, table[XS, e], table[ZS, e], table[CORES, e])
                 block = jnp.where(table[HALF, e] == n % 2, block, pltpu.roll(block, BLK, 1))
                 stack.append(jnp.where(lanes == n % 2, block, 0.0))
             high, low = split(jnp.concatenate(stack, axis=0))
             both = dot(high, wide)
             made = both[:, :TWO] + both[:, TWO:] + dot(low, high_w)
             for n in range(8):
-                term = jnp.where(side == n // 4, made[n * CP : (n + 1) * CP], 0.0)
-                first[q * 8 + n] = term + first[table[PREV1 + n % 2, ((n // 2) << bits) + q]]
+                term = jnp.where(side == n // 4, made[n * cp : (n + 1) * cp], 0.0)
+                first[q * 8 + n, :cp, :] = term + first[table[PREV1 + n % 2, ((n // 2) << bits) + q], :cp, :]
             return 0
 
         lax.fori_loop(0, NY, one_panel, 0)
 
         def one_column(j, _):
-            parts[h][y, j] = first[table[LAST1, j]] * keep[pl.ds(j, 1), :]
+            parts[h][y, j] = first[table[LAST1, j], :cp, :] * keep[pl.ds(j, 1), :]
             return 0
 
         lax.fori_loop(0, per, one_column, 0)
 
-    quarter = BLK // 2
-
-    def half_pass(q, half, fresh):
-        here = range(half * NP // 2, (half + 1) * NP // 2)
-        inside = (iota((TWO, TWO), 1) % BLK) // quarter == half
-
+    def second_pass(q, fresh):
         def one_device(d, _):
             device = q * (per // 2) + d
-            block = jnp.concatenate([panel[h][device // 2, device % 2, : 2 * CP, :] for h in range(NP)], axis=0)
-            high = block.astype(BF16)
-            rough = high.astype(F32)
-            rest = pltpu.roll(block - rough, quarter if half == 0 else TWO - quarter, 1)
-            mixed = jnp.where(inside, rough, rest).astype(BF16)
+            spot = (device // (2 * NZ), (device // 2) % NZ, device % 2)
+            high, low = split(jnp.concatenate([block_of(h, *spot) for h in range(NP)], axis=0))
             none = jnp.zeros((BLK, TWO), BF16)
-            blank = jnp.zeros((quarter, TWO), BF16)
             upper, lower = [], []
             for r in range(2):
-                high_w, low_w = split(jnp.concatenate([parts[h][q, d * 2 + r] for h in here], axis=0))
-                twice = jnp.concatenate([high_w, high_w], axis=0)
-                once = jnp.concatenate([low_w, blank] if half == 0 else [blank, low_w], axis=0)
-                upper.append(jnp.concatenate([twice, none] if r == 0 else [none, twice], axis=1))
-                lower.append(jnp.concatenate([once, none] if r == 0 else [none, once], axis=1))
-            made = dot(jnp.concatenate([mixed, high], axis=1), jnp.concatenate(upper + lower, axis=0))
+                pieces = split(jnp.concatenate([parts[h][q, d * 2 + r] for h in range(NP)], axis=0))
+                for side, piece in zip((upper, lower), pieces):
+                    side.append(jnp.concatenate([piece, none] if r == 0 else [none, piece], axis=1))
+            made = dot(jnp.concatenate([high, low], axis=1), jnp.concatenate(upper + upper, axis=0))
+            made = made + dot(high, jnp.concatenate(lower, axis=0))
             for r in range(2):
                 for s in range(2):
                     term = jnp.concatenate(
-                        [made[(h * 2 + s) * CP : (h * 2 + s + 1) * CP, r * TWO : (r + 1) * TWO] for h in range(NP)],
+                        [
+                            made[2 * AT[h] + s * WIDTHS[h] : 2 * AT[h] + (s + 1) * WIDTHS[h], r * TWO : (r + 1) * TWO]
+                            for h in range(NP)
+                        ],
                         axis=0,
                     )
                     second[d * 4 + r * 2 + s] = term + second[table[PREV2 + r * 2 + s, device]]
@@ -361,33 +396,36 @@
     def own(pair):
         return jnp.concatenate([parts[h][y, pair * 2 + b] for b in range(2) for h in range(NP)], axis=0)
 
-    def arrived(hop, half):
-        half_pass((y + NY - hop) % NY, half, False)
-        if 2 * hop < NY:
-            half_pass((y + hop) % NY, half, False)
-
-    for tick in range(NP + near):
-        if 1 <= tick < NP:
-            x_end(tick)
-        if tick < NP:
-            first_part(tick)
-            y_step(tick, 0)
-        if tick + 1 < NP:
-            x_middle(tick + 1)
-        for hop in range(1, near + 1):
-            if 0 <= tick - hop < NP:
-                y_step(tick - hop, hop)
-        if tick == NP - 1:
-            half_pass(y, 0, True)
-            arrived(1, 0)
-        if NP <= tick <= NP + near - 2:
-            arrived(tick - NP + 2, 0)
-        if tick == NP:
-            half_pass(y, 1, False)
+    def arrive(*steps):
+        for h, hop in steps:
+            y_step(h, hop)
+
+    def form(h):
+        first_part(h)
+        y_step(h, 0)
+
+    form(0)
+    w_step(5)
+    x_middle(1)
+    for hop in range(6, NZ // 2 + 1):
+        w_step(hop)
+    x_end(1)
+    form(1)
+    w_end()
+    form(2)
+    arrive((0, 1))
+    form(3)
+    arrive((1, 1))
+    second_pass(y, True)
+    for hop in range(1, near + 1):
+        if hop > 1:
+            arrive((0, hop), (1, hop))
+            second_pass((y + hop - 1) % NY, False)
+        if hop == near:
             for pair in range(per // 2):
                 square[:, pair * TWO : (pair + 1) * TWO] = own(pair).T
-        if tick >= NP:
-            arrived(tick - NP + 1, 1)
+        arrive((2, hop), (3, hop))
+        second_pass((y + NY - hop) % NY, False)
     for pair in range(per // 2):
         cube = jnp.concatenate(
             [total[pair * 2 + b] * keep[pair * 2 + b : pair * 2 + b + 1, :] for b in range(2)], axis=0
@@ -405,11 +443,13 @@
     def dma(*shape):
         return [pltpu.SemaphoreType.DMA(shape), pltpu.SemaphoreType.DMA(shape)]
 
+    held = AHEAD + 1
+
     def body(ids, counts, tile, keep_pattern, square, purified, *rest):
-        panel, parts, others, sems = rest[:NP], rest[NP : 2 * NP], rest[2 * NP : 2 * NP + 10], rest[2 * NP + 10 :]
-        pairs = [sems[2 * n : 2 * n + 2] for n in range(5)]
+        panel, parts, others, sems = rest[:held], rest[held : held + NP], rest[held + NP : held + NP + 9], rest[held + NP + 9 :]
+        pairs = [sems[2 * n : 2 * n + 2] for n in range(7)]
         purify(
-            per, ids, counts, tile, keep_pattern, square, purified, panel, parts, *others, *pairs, sems[10], sems[11]
+            per, ids, counts, tile, keep_pattern, square, purified, panel, parts, *others, *pairs, sems[14], sems[15]
         )
 
     out = jax.ShapeDtypeStruct((TWO, per * BLK), F32)
@@ -418,13 +458,13 @@
         out_shape=(out, out),
         in_specs=[vmem] * 4,
         out_specs=(vmem, vmem),
-        scratch_shapes=[pltpu.VMEM((NX * NZ, 2, part_rows(h), TWO), F32) for h in range(NP)]
-        + [pltpu.VMEM((NY, per, CP, TWO), F32) for _ in range(NP)]
+        scratch_shapes=[pltpu.VMEM((NX, NZ, 2, part_rows(h), TWO), F32) for h in range(AHEAD)]
+        + [pltpu.VMEM((NX, NZ, 2, sum(part_rows(h) for h in range(AHEAD, NP)), TWO), F32)]
+        + [pltpu.VMEM((NY, per, WIDTHS[h], TWO), F32) for h in range(NP)]
         + [
             pltpu.VMEM((NY, TWO + EXTRA, TWO), F32),
-            pltpu.VMEM((NZ, 2 * CP * AHEAD + EXTRA, TWO), F32),
-            pltpu.VMEM((NZ, 2 * CP * (NP - AHEAD), TWO), F32),
-            pltpu.VMEM((8 * NY + 1, CP, TWO), F32),
+            pltpu.VMEM((NZ, sum(part_rows(h) for h in range(AHEAD)), TWO), F32),
+            pltpu.VMEM((8 * NY + 1, max(WIDTHS), TWO), F32),
             pltpu.VMEM((2 * per + 1, BLK, TWO), F32),
             pltpu.VMEM((per, BLK, TWO), F32),
             pltpu.VMEM((per, TWO), F32),
@@ -432,8 +472,8 @@
             pltpu.VMEM((TABLE, TWO), I32),
             pltpu.SMEM((TABLE, TWO), I32),
         ]
-        + dma(2, 2, NZ) + dma(2, NY) + dma(NP, 3) + dma(NP, 4) + dma(NP, 2, NY)
-        + [pltpu.SemaphoreType.DMA((NP,)), pltpu.SemaphoreType.DMA],
+        + dma(2, 2, NZ) + dma(2, NY) + dma(AHEAD, 3) + dma(AHEAD, 4) + dma(NP, 2, NY) + dma(3) + dma(NZ)
+        + [pltpu.SemaphoreType.DMA((AHEAD,)), pltpu.SemaphoreType.DMA],
         compiler_params=pltpu.CompilerParams(collective_id=0, has_side_effects=True, vmem_limit_bytes=48 << 20),
         name="purify",
     )(column_ids, counts, values, keep_pattern)

time: 160 us -> 133 us (0.83)
  Pallas kernels: 155 us -> 128 us
    pallas_call x1, Pallas kernels: 155 us -> 128 us  [local(): pl.pallas_call(body, out_shape=(out, out), in_specs=[vmem] * 4, out_specs...]
where the time goes in v3:
time: 133 us
  Pallas kernels  128 us (96%)
  local copies, waits for them, and re-layouts  4.03 us (3%)
    pallas_call x1, Pallas kernels, local(): pl.pallas_call(body, out_shape=(out, out), in_specs=[vmem] * 4, out_specs...  128 us
    unnamed x9, local copies, waits for them, and re-layouts  4.03 us

profile of v3, /device:TPU:1, one launch (start us, length us, event | category | flops | bytes accessed | tf_op | source)
XLA Modules:
  0.0 132.7 jit_solution(8624616803365505157)
XLA Ops:
  0.6 0.0 copy-start.1
  0.6 0.7 copy.6.counts
  1.4 0.0 copy-done.1
  1.4 0.0 copy-start
  1.4 0.8 copy-done
  2.2 0.0 copy-start.2
  2.2 0.7 copy-done.2
  2.9 128.0 %purify.1 = (f32[128,1536]{1,0:T(8,128)S(1)}, f32[128,1536]{1,0:T(8,128)S(1)}) custom-call(s32[2,2]{1,0:T(2,128)S(1)} %copy-done.1, s32[2,1]{1,0:T(2,128)S(1)} %copy.6.counts, f32[128,128]{1,0:T(8,128)S(1)} %copy-done, s32[2,24]{1,0:T(2,128)S(1)} %copy-done.2), custom_call_target="tpu_custom_call" | custom-call | tf_op jit(solution)/shard_map/purify/pallas_call | solution.py:456
  130.9 0.9 copy.9
  131.8 0.9 copy.10
Async XLA Ops:
  0.6 0.8 copy-start.1
  1.4 0.8 copy-start
  2.2 0.7 copy-start.2

commit v4 on v3

--- a/solution.py
+++ b/solution.py
@@ -137,7 +137,7 @@
 def purify(
     per, ids, counts, tile, keep_pattern, square, purified,
     panel, parts, row, early, first, second, total, keep, tags, table_v, table,
-    z_sems, r_sems, x_sems, s_sems, y_sems, w_sems, t_sems, own_sem, table_sem,
+    z_sems, r_sems, x_sems, s_sems, y_sems, w_sems, t_sems, c_sems, own_sem, table_sem,
 ):
     x, z, core, y = place()
     west, east = (z + NZ - 1) % NZ, (z + 1) % NZ
@@ -160,7 +160,7 @@
 
     def z_copy(g, way, hop):
         slot = (z + NZ - hop) % NZ if way == 0 else (z + hop) % NZ
-        ref = early.at[slot] if g == 0 else wide.at[:, slot, core]
+        ref = (panel[0].at[x, slot, core], wide.at[:, slot, core], early.at[slot])[g]
         return send(ref, ref, z_sems, (g, way, hop), to(x, east if way == 0 else west, core, y))
 
     def z_step(g, hop):
@@ -192,7 +192,7 @@
         return panel[h].at[at, :, core]
 
     def source(h):
-        at = sum(part_rows(g) for g in range(h))
+        at = sum(part_rows(g) for g in range(1, h))
         return early.at[:, at : at + part_rows(h)]
 
     def x_copy(h, n):
@@ -207,9 +207,9 @@
         return pltpu.make_async_copy(source(h), slab(h, x), own_sem.at[h])
 
     def s_copy(h, n):
-        if n == 0:
+        if n == 0 and h > 0:
             return send(source(h), slab(h, x), s_sems, (h, 0), twin)
-        held = slab(h, (before, after, (x + 2) % NX)[n - 1])
+        held = slab(h, (x, before, after, (x + 2) % NX)[n])
         return send(held, held, s_sems, (h, n), twin)
 
     def x_begin(h):
@@ -231,6 +231,28 @@
         own_copy(h).wait()
         for n in range(4):
             s_copy(h, n).wait_recv()
+
+    def c_copy(n, k):
+        at = (x, x, jnp.where(core == 0, before, after))[k]
+        target = (after, before, jnp.where(core == 0, after, before))[k]
+        ref = panel[0].at[at, (z + NZ - n) % NZ, core]
+        return send(ref, ref, c_sems, (n, k), to(target, z, core, y))
+
+    def chunks(hop):
+        if hop == 0:
+            return [0]
+        return [n for way, n in ((0, hop), (1, NZ - hop)) if hop <= z_hops[way]]
+
+    def spread(hop):
+        for n in chunks(hop):
+            for k in range(2):
+                start(c_copy(n, k))
+
+    def relay(hop):
+        for n in chunks(hop):
+            for k in range(2):
+                c_copy(n, k).wait_recv()
+            start(c_copy(n, 2))
 
     def w_copy(n):
         at = (x, x, jnp.where(core == 0, before, after))[n]
@@ -271,14 +293,18 @@
     for h in range(NP):
         for s in range(2):
             chunk = held[s * BLK + AT[h] : s * BLK + AT[h] + WIDTHS[h]]
-            if h < AHEAD:
-                at = sum(part_rows(g) for g in range(h)) + s * WIDTHS[h]
+            if h == 0:
+                panel[0][x, z, core, s * WIDTHS[0] : (s + 1) * WIDTHS[0]] = chunk
+            elif h < AHEAD:
+                at = sum(part_rows(g) for g in range(1, h)) + s * WIDTHS[h]
                 early[z, at : at + WIDTHS[h]] = chunk
             else:
                 at = ROWS[h] + s * WIDTHS[h]
                 wide[x, z, core, at : at + WIDTHS[h]] = chunk
-    early[z, 2 * WIDTHS[0] : 2 * WIDTHS[0] + EXTRA] = mark
+    panel[0][x, z, core, 2 * WIDTHS[0] :] = mark
     z_step(0, 0)
+    spread(0)
+    z_step(2, 0)
     r_step(0)
     for n in range(2):
         start(w_copy(n))
@@ -293,6 +319,10 @@
 
     for hop in range(1, max(NZ // 2, near) + 1):
         z_step(0, hop)
+        spread(hop)
+        if hop <= NZ // 2:
+            relay(hop - 1)
+        z_step(2, hop)
         r_step(hop)
         if hop == 1:
             for n in range(2):
@@ -301,14 +331,20 @@
         if hop == 2:
             w_copy(2).wait_recv()
             w_step(0)
-        if hop in (4, 5):
-            w_step(hop - 3)
-    x_begin(0)
+        if hop == 4:
+            w_step(1)
+    start(s_copy(0, 0))
+    relay(NZ // 2)
+    for n in range(1, 3):
+        start(s_copy(0, n))
+    x_begin(1)
+    w_step(2)
+    for n in range(NZ):
+        c_copy(n, 2).wait_recv()
+    start(s_copy(0, 3))
     w_step(3)
-    x_middle(0)
-    x_begin(1)
-    w_step(4)
-    x_end(0)
+    for n in range(4):
+        s_copy(0, n).wait_recv()
 
     def tag_row(n, _):
         for c in range(2):
@@ -404,28 +440,41 @@
         first_part(h)
         y_step(h, 0)
 
+    def run(hop, way):
+        if hop <= near and (way == 0 or 2 * hop < NY):
+            second_pass((y + NY - hop) % NY if way == 0 else (y + hop) % NY, False)
+
     form(0)
+    w_step(4)
+    x_middle(1)
     w_step(5)
-    x_middle(1)
+    arrive((0, 1))
+    x_end(1)
+    form(1)
+    arrive((0, 2))
     for hop in range(6, NZ // 2 + 1):
         w_step(hop)
-    x_end(1)
-    form(1)
     w_end()
     form(2)
-    arrive((0, 1))
+    arrive((1, 1))
     form(3)
-    arrive((1, 1))
     second_pass(y, True)
-    for hop in range(1, near + 1):
-        if hop > 1:
-            arrive((0, hop), (1, hop))
-            second_pass((y + hop - 1) % NY, False)
-        if hop == near:
-            for pair in range(per // 2):
-                square[:, pair * TWO : (pair + 1) * TWO] = own(pair).T
-        arrive((2, hop), (3, hop))
-        second_pass((y + NY - hop) % NY, False)
+    arrive((0, 3), (2, 1), (1, 2), (3, 1))
+    run(1, 1)
+    arrive((0, 4), (2, 2))
+    run(1, 0)
+    arrive((1, 3), (3, 2))
+    run(2, 1)
+    arrive((2, 3))
+    run(2, 0)
+    arrive((1, 4), (3, 3))
+    run(3, 1)
+    arrive((2, 4))
+    run(3, 0)
+    for pair in range(per // 2):
+        square[:, pair * TWO : (pair + 1) * TWO] = own(pair).T
+    arrive((3, 4))
+    run(4, 0)
     for pair in range(per // 2):
         cube = jnp.concatenate(
             [total[pair * 2 + b] * keep[pair * 2 + b : pair * 2 + b + 1, :] for b in range(2)], axis=0
@@ -447,9 +496,9 @@
 
     def body(ids, counts, tile, keep_pattern, square, purified, *rest):
         panel, parts, others, sems = rest[:held], rest[held : held + NP], rest[held + NP : held + NP + 9], rest[held + NP + 9 :]
-        pairs = [sems[2 * n : 2 * n + 2] for n in range(7)]
+        pairs = [sems[2 * n : 2 * n + 2] for n in range(8)]
         purify(
-            per, ids, counts, tile, keep_pattern, square, purified, panel, parts, *others, *pairs, sems[14], sems[15]
+            per, ids, counts, tile, keep_pattern, square, purified, panel, parts, *others, *pairs, sems[16], sems[17]
         )
 
     out = jax.ShapeDtypeStruct((TWO, per * BLK), F32)
@@ -463,7 +512,7 @@
         + [pltpu.VMEM((NY, per, WIDTHS[h], TWO), F32) for h in range(NP)]
         + [
             pltpu.VMEM((NY, TWO + EXTRA, TWO), F32),
-            pltpu.VMEM((NZ, sum(part_rows(h) for h in range(AHEAD)), TWO), F32),
+            pltpu.VMEM((NZ, sum(part_rows(h) for h in range(1, AHEAD)), TWO), F32),
             pltpu.VMEM((8 * NY + 1, max(WIDTHS), TWO), F32),
             pltpu.VMEM((2 * per + 1, BLK, TWO), F32),
             pltpu.VMEM((per, BLK, TWO), F32),
@@ -472,7 +521,7 @@
             pltpu.VMEM((TABLE, TWO), I32),
             pltpu.SMEM((TABLE, TWO), I32),
         ]
-        + dma(2, 2, NZ) + dma(2, NY) + dma(AHEAD, 3) + dma(AHEAD, 4) + dma(NP, 2, NY) + dma(3) + dma(NZ)
+        + dma(3, 2, NZ) + dma(2, NY) + dma(AHEAD, 3) + dma(AHEAD, 4) + dma(NP, 2, NY) + dma(3) + dma(NZ) + dma(NZ, 3)
         + [pltpu.SemaphoreType.DMA((AHEAD,)), pltpu.SemaphoreType.DMA],
         compiler_params=pltpu.CompilerParams(collective_id=0, has_side_effects=True, vmem_limit_bytes=48 << 20),
         name="purify",

time: 133 us -> 128 us (0.962)
  Pallas kernels: 128 us -> 123 us
    pallas_call x1, Pallas kernels: 128 us -> 123 us  [local(): pl.pallas_call(body, out_shape=(out, out), in_specs=[vmem] * 4, out_specs...]
where the time goes in v4:
time: 128 us
  Pallas kernels  123 us (96%)
  local copies, waits for them, and re-layouts  4.03 us (3%)
    pallas_call x1, Pallas kernels, local(): pl.pallas_call(body, out_shape=(out, out), in_specs=[vmem] * 4, out_specs...  123 us
    unnamed x9, local copies, waits for them, and re-layouts  4.03 us

profile of v4, /device:TPU:1, one launch (start us, length us, event | category | flops | bytes accessed | tf_op | source)
XLA Modules:
  0.0 127.9 jit_solution(9453469877473332287)
XLA Ops:
  0.6 0.0 copy-start.1
  0.6 0.7 copy.6.counts
  1.4 0.0 copy-done.1
  1.4 0.0 copy-start
  1.4 0.8 copy-done
  2.2 0.0 copy-start.2
  2.2 0.7 copy-done.2
  2.9 123.2 %purify.1 = (f32[128,1536]{1,0:T(8,128)S(1)}, f32[128,1536]{1,0:T(8,128)S(1)}) custom-call(s32[2,2]{1,0:T(2,128)S(1)} %copy-done.1, s32[2,1]{1,0:T(2,128)S(1)} %copy.6.counts, f32[128,128]{1,0:T(8,128)S(1)} %copy-done, s32[2,24]{1,0:T(2,128)S(1)} %copy-done.2), custom_call_target="tpu_custom_call" | custom-call | tf_op jit(solution)/shard_map/purify/pallas_call | solution.py:505
  126.1 0.9 copy.9
  127.0 0.9 copy.10
Async XLA Ops:
  0.6 0.8 copy-start.1
  1.4 0.8 copy-start
  2.2 0.7 copy-start.2

commit v5 on v4

--- a/solution.py
+++ b/solution.py
@@ -135,9 +135,9 @@
 
 
 def purify(
-    per, ids, counts, tile, keep_pattern, square, purified,
+    per, given, ids, counts, tile, keep_pattern, square, purified,
     panel, parts, row, early, first, second, total, keep, tags, table_v, table,
-    z_sems, r_sems, x_sems, s_sems, y_sems, w_sems, t_sems, c_sems, own_sem, table_sem,
+    z_sems, r_sems, x_sems, s_sems, y_sems, w_sems, t_sems, c_sems, own_sem, table_sem, load_sem,
 ):
     x, z, core, y = place()
     west, east = (z + NZ - 1) % NZ, (z + 1) % NZ
@@ -274,13 +274,21 @@
         for n in range(NZ):
             t_copy(n, z).wait_recv()
 
+    loads = [
+        pltpu.make_async_copy(src, dst, load_sem.at[n])
+        for n, (src, dst) in enumerate(zip(given, (ids, counts, tile, keep_pattern)))
+    ]
+    for load in loads:
+        load.start()
     greet(
         [to(after, z, core, y), to(before, z, core, y), to(x, west, core, y), to(x, east, core, y)]
         + [twin, to(x, z, core, south), to(x, z, core, north)]
     )
 
+    for load in loads:
+        load.wait()
     at_row, at_lane = iota((TWO, TWO), 0), iota((TWO, TWO), 1)
-    live = jnp.where(at_row < BLK, counts[0:1, 0:1], counts[1:2, 0:1])
+    live = jnp.where(at_row < BLK, counts[0:1, 0:1], counts[0:1, 1:2])
     held = jnp.where((at_lane >= BLK).astype(I32) < live, tile[...], 0.0).T
     lane = iota((EXTRA, TWO), 1)
     mark = jnp.where(
@@ -494,20 +502,24 @@
 
     held = AHEAD + 1
 
-    def body(ids, counts, tile, keep_pattern, square, purified, *rest):
+    inputs = (((2, 2), I32), ((1, 2), I32), ((TWO, TWO), F32), ((2, per), I32))
+
+    def body(*refs):
+        given, (square, purified), loaded, rest = refs[:4], refs[4:6], refs[6:10], refs[10:]
         panel, parts, others, sems = rest[:held], rest[held : held + NP], rest[held + NP : held + NP + 9], rest[held + NP + 9 :]
         pairs = [sems[2 * n : 2 * n + 2] for n in range(8)]
         purify(
-            per, ids, counts, tile, keep_pattern, square, purified, panel, parts, *others, *pairs, sems[16], sems[17]
+            per, given, *loaded, square, purified, panel, parts, *others, *pairs, *sems[16:]
         )
 
     out = jax.ShapeDtypeStruct((TWO, per * BLK), F32)
     return pl.pallas_call(
         body,
         out_shape=(out, out),
-        in_specs=[vmem] * 4,
+        in_specs=[pl.BlockSpec(memory_space=pltpu.HBM)] * 4,
         out_specs=(vmem, vmem),
-        scratch_shapes=[pltpu.VMEM((NX, NZ, 2, part_rows(h), TWO), F32) for h in range(AHEAD)]
+        scratch_shapes=[pltpu.VMEM(*shape) for shape in inputs]
+        + [pltpu.VMEM((NX, NZ, 2, part_rows(h), TWO), F32) for h in range(AHEAD)]
         + [pltpu.VMEM((NX, NZ, 2, sum(part_rows(h) for h in range(AHEAD, NP)), TWO), F32)]
         + [pltpu.VMEM((NY, per, WIDTHS[h], TWO), F32) for h in range(NP)]
         + [
@@ -522,10 +534,10 @@
             pltpu.SMEM((TABLE, TWO), I32),
         ]
         + dma(3, 2, NZ) + dma(2, NY) + dma(AHEAD, 3) + dma(AHEAD, 4) + dma(NP, 2, NY) + dma(3) + dma(NZ) + dma(NZ, 3)
-        + [pltpu.SemaphoreType.DMA((AHEAD,)), pltpu.SemaphoreType.DMA],
-        compiler_params=pltpu.CompilerParams(collective_id=0, has_side_effects=True, vmem_limit_bytes=48 << 20),
+        + [pltpu.SemaphoreType.DMA((AHEAD,)), pltpu.SemaphoreType.DMA, pltpu.SemaphoreType.DMA((4,))],
+        compiler_params=pltpu.CompilerParams(collective_id=0, has_side_effects=True, vmem_limit_bytes=63 << 20),
         name="purify",
-    )(column_ids, counts, values, keep_pattern)
+    )(column_ids, counts.reshape(1, 2), values, keep_pattern)
 
 
 def solution(mesh):

time: 128 us -> 128 us (level)
    unnamed x9 -> x4, local copies, waits for them, and re-layouts: 4.03 us -> 3.03 us
where the time goes in v5:
time: 128 us
  Pallas kernels  124 us (97%)
  local copies, waits for them, and re-layouts  3.03 us (2%)
    pallas_call x1, Pallas kernels, local(): pl.pallas_call(body, out_shape=(out, out), in_specs=[pl.BlockSpec(memory_...  124 us
    unnamed x4, local copies, waits for them, and re-layouts  3.03 us

profile of v5, /device:TPU:1, one launch (start us, length us, event | category | flops | bytes accessed | tf_op | source)
XLA Modules:
  0.0 128.1 jit_solution(15276681204611991239)
XLA Ops:
  0.6 124.4 %purify.1 = (f32[128,1536]{1,0:T(8,128)}, f32[128,1536]{1,0:T(8,128)}) custom-call(s32[2,2]{1,0:T(2,128)} %refs_0_.1, s32[1,2]{1,0:T(1,128)} %bitcast.1, f32[128,128]{1,0:T(8,128)} %refs_2_.1, s32[2,24]{1,0:T(2,128)} %refs_3_.1), custom_call_target="tpu_custom_call" | custom-call | tf_op jit(solution)/shard_map/purify/pallas_call | solution.py:516
  125.0 0.0 copy-start
  125.0 2.1 %copy.8 = f32[128,1536]{1,0:T(8,128)} copy(f32[128,1536]{1,0:T(8,128)} %get-tuple-element.4) | data formatting | bytes 1572864
  127.2 0.0 copy-done
  127.2 0.9 copy.9
Async XLA Ops:
  125.0 2.2 %copy-start = (f32[128,1536]{1,0:T(8,128)S(1)}, f32[128,1536]{1,0:T(8,128)}, u32[]{:S(2)}) copy-start(f32[128,1536]{1,0:T(8,128)} %get-tuple-element.5) | copy-start | bytes 2359300
